TPU v7x, 32 devices: a whole 2x2x4 slice. The times are simulated.
32 devices in a mesh: dp: 4 (over x, core), code: 8 (over z, y).
Axes of the slice: x: 2, y: 2, z: 4, core: 2. Of those that a mesh axis runs over, the one named last changes fastest.
Arguments:
- latents: bfloat16 [2048, 256], P(('dp', 'code')), may hold values from -1000 to 1000
- out_grad: bfloat16 [2048, 256], P(('dp', 'code')), may hold values from -6 to 6
- targets: int32 [2048], P('dp'), may hold values from 0 to 65535
- codebook: bfloat16 [65536, 256], P('code'), may hold values from -2 to 2
Outputs:
- latent_grad: bfloat16 [2048, 256], P(('dp', 'code'))
- codebook_grad: float32 [65536, 256], P(('code', 'dp'))
- token_loss: float32 [2048], P(('dp', 'code'))
All inputs are finite; a program needn't handle non-finite values.
Results may differ from a plain program's by a relative error of at most 0.0042.
Values may be sent and summed in bfloat16 or wider, within the bound.
A program may use at most 128 MiB of HBM per device.

v0:
```python
import jax
import jax.numpy as jnp
from jax import lax
from jax.sharding import PartitionSpec as P

ce_weight = 1.0


def per_device(latents, out_grad, targets, codebook):
    lat_all, grad_all = (
        lax.all_gather(latents, "code", axis=0, tiled=True),
        lax.all_gather(out_grad, "code", axis=0, tiled=True),
    )
    code_dev, feature_width = codebook.shape
    groups = lax.axis_size("dp")
    blocks = max(1, code_dev // 2048)
    sub_rows = code_dev // groups
    block_rows = sub_rows // blocks
    local_ids = targets - lax.axis_index("code") * code_dev
    layered = codebook.reshape(groups, blocks, block_rows, feature_width)
    dims_nt = (((1,), (1,)), ((), ()))

    def block_parts(block):
        book_block = layered[:, block].reshape(groups * block_rows, feature_width)
        code_ids = (
            jnp.arange(groups, dtype=jnp.int32)[:, None] * sub_rows
            + block * block_rows
            + jnp.arange(block_rows, dtype=jnp.int32)[None, :]
        ).reshape(-1)
        hit_mask = local_ids[:, None] == code_ids[None, :]
        logit_block = lax.dot_general(
            lat_all, book_block, dims_nt, preferred_element_type=jnp.float32
        )
        back_block = lax.dot_general(
            grad_all, book_block, dims_nt, preferred_element_type=jnp.float32
        )
        return (book_block, hit_mask, logit_block, back_block)

    tok_count = lat_all.shape[0]
    top = jnp.full((tok_count,), -jnp.inf, jnp.float32)
    total = jnp.zeros((tok_count,), jnp.float32)
    weighted = jnp.zeros((tok_count,), jnp.float32)
    picked = jnp.zeros((tok_count,), jnp.float32)
    for block in range(blocks):
        book_block, hit_mask, logit_block, back_block = block_parts(block)
        new_top = jnp.maximum(top, jnp.max(logit_block, axis=1))
        factor = jnp.exp(top - new_top)
        expo = jnp.exp(logit_block - new_top[:, None])
        total = total * factor + jnp.sum(expo, axis=1)
        weighted = weighted * factor + jnp.sum(expo * back_block, axis=1)
        picked = picked + jnp.sum(jnp.where(hit_mask, logit_block, 0.0), axis=1)
        top = new_top
    peak_value = lax.pmax(top, "code")
    rescale = jnp.exp(top - peak_value)
    total, weighted, picked = lax.psum((total * rescale, weighted * rescale, picked), "code")
    lse = peak_value + jnp.log(total)
    mean_back = weighted / total
    own_count = latents.shape[0]
    token_loss = lax.dynamic_slice_in_dim(
        lse - picked, lax.axis_index("code") * own_count, own_count, 0
    )
    valid = (local_ids >= 0) & (local_ids < code_dev)
    segment_ids = jnp.where(valid, local_ids, code_dev)
    direct = jax.ops.segment_sum(
        grad_all.astype(jnp.float32), segment_ids, num_segments=code_dev + 1
    )[:code_dev]
    direct = direct.reshape(groups, blocks, block_rows, feature_width)
    lat_grad = jnp.zeros((tok_count, feature_width), jnp.float32)
    collected = []
    for block in range(blocks):
        book_block, hit_mask, logit_block, back_block = block_parts(block)
        probs = jnp.exp(logit_block - lse[:, None])
        delta = probs * (back_block - mean_back[:, None]) + ce_weight * (
            probs - hit_mask.astype(jnp.float32)
        )
        delta = delta.astype(jnp.bfloat16)
        lat_grad = lat_grad + jnp.dot(delta, book_block, preferred_element_type=jnp.float32)
        term = lax.dot_general(
            delta, lat_all, (((0,), (0,)), ((), ())), preferred_element_type=jnp.float32
        )
        term = term + direct[:, block].reshape(groups * block_rows, feature_width)
        collected.append(term.reshape(groups, 1, block_rows, feature_width))
    whole = jnp.concatenate(collected, axis=1).reshape(code_dev, feature_width)
    codebook_grad = lax.psum_scatter(whole, "dp", scatter_dimension=0, tiled=True)
    latent_grad = lax.psum_scatter(lat_grad, "code", scatter_dimension=0, tiled=True).astype(
        jnp.bfloat16
    )
    return (latent_grad, codebook_grad, token_loss)


def solution(mesh):
    in_specs = (P(("dp", "code"), None), P(("dp", "code"), None), P("dp"), P("code", None))
    out_specs = (P(("dp", "code"), None), P(("code", "dp"), None), P(("dp", "code")))
    return jax.shard_map(
        per_device, mesh=mesh, in_specs=in_specs, out_specs=out_specs, check_vma=False
    )
```

profile of v0, /device:TPU:0, one launch (start us, length us, event | category | flops | bytes accessed | tf_op | source)
XLA Modules:
  0.0 308.3 jit_solution(16452300999294263003)
XLA Ops:
  7.2 0.0 reduce-scatter.3.cloned.1.call-start
  7.3 32.8 %all_gather.6 = bf16[512,256]{1,0:T(8,128)(2,1)S(1)} all-gather(bf16[64,256]{1,0:T(8,128)(2,1)} %param.4), channel_id=1, replica_groups=mesh['dp'=4,'code'=8] {'code'}, dimensions={0}, use_global_device_ids=true | all-gather | bytes 294912 | tf_op jit(solution)/shard_map/all_gather | solution.py:11
  40.0 30.9 %all_gather.7 = bf16[512,256]{1,0:T(8,128)(2,1)S(1)} all-gather(bf16[64,256]{1,0:T(8,128)(2,1)} %param.5), channel_id=1, replica_groups=mesh['dp'=4,'code'=8] {'code'}, dimensions={0}, use_global_device_ids=true | all-gather | bytes 294912 | tf_op jit(solution)/shard_map/all_gather | solution.py:12
  71.0 3.5 %fusion.26 = (bf16[4,1,512,256]{3,2,1,0:T(8,128)(2,1)S(1)}, bf16[4,1,512,256]{3,2,1,0:T(8,128)(2,1)S(1)}, bf16[4,1,512,256]{3,2,1,0:T(8,128)(2,1)S(1)}, bf16[4,1,512,256]{3,2,1,0:T(8,128)(2,1)}) fusion(bf16[4,4,512,256]{3,2,1,0:T(8,128)(2,1)} %bitcast.78), kind=kLoop, calls=%fused_computation.70 | loop fusion | bytes 8388608 | tf_op jit(solution)/shard_map/slice | solution.py:24
  74.5 2.7 fusion.33
  77.1 2.7 fusion.31
  79.8 2.7 fusion.28
  82.6 0.0 copy-done.8
  82.6 2.7 fusion.30
  85.2 0.0 copy-done.9
  85.2 2.7 fusion.32
  88.0 2.7 fusion.29
  90.7 0.1 add_bitcast_fusion.3
  90.7 0.1 add_bitcast_fusion
  90.8 0.1 add_bitcast_fusion.1
  90.9 0.1 add_bitcast_fusion.2
  91.0 0.0 copy-done.11
  91.0 2.7 fusion.27
  93.7 21.4 %pmax.7 = f32[512]{0:T(512)S(1)} all-reduce(f32[512]{0:T(512)S(1)} %get-tuple-element.22), channel_id=1, replica_groups=mesh['dp'=4,'code'=8] {'code'}, use_global_device_ids=true, to_apply=%region_4.5 | all-reduce | flops 512 | bytes 4096 | tf_op jit(solution)/shard_map/pmax | solution.py:53
  115.1 0.0 copy-done.10
  115.1 13.2 %fusion.18 = (f32[512]{0:T(512)S(1)}, f32[512]{0:T(512)S(1)}, f32[512]{0:T(512)S(1)}, f32[512]{0:T(512)S(1)}, f32[512]{0:T(512)S(1)}, /*index=5*/f32[512]{0:T(51...) fusion(f32[512,2048]{1,0:T(8,128)} %get-tuple-element.50, ...), kind=kOutput, calls=%fused_computation.36 | convolution fusion | flops 566224896 | bytes 34932736 | tf_op jit(solution)/shard_map/dot_general | solution.py:34
  128.3 17.5 %all-reduce = (f32[512]{0:T(512)S(1)}, f32[512]{0:T(512)S(1)}, f32[512]{0:T(512)S(1)}) all-reduce(f32[512]{0:T(512)S(1)} %get-tuple-element.34, f32[512]{0:T(512)S(1)} %get-tuple-element.33, f32[512]{0:T(512)S(1)} %add_add_fusion), channel_id=1, replica_groups=mesh['dp'=4,'code'=8] {'code'}, use_global_device_ids=true, to_apply=%region_14.15 | all-reduce | flops 1536 | bytes 12288 | tf_op jit(solution)/shard_map/psum | solution.py:55
  145.9 13.5 %fusion.16 = (bf16[512,2048]{1,0:T(8,128)(2,1)S(1)}, bf16[512,2048]{1,0:T(8,128)(2,1)S(1)}, bf16[512,2048]{1,0:T(8,128)(2,1)S(1)}, bf16[512,2048]{1,0:T(8,128)(2,1)S(1)}) fusion(f32[512,2048]{1,0:T(8,128)} %fusion.33, f32[512,2048]{1,0:T(8,128)} %get-tuple-element.52, s32[2048]{0:T(1024)S(1)} %bitcast.85, f32[512]{0:T(512)S(1)} %get-tuple-element.39, ...), kind=kLoop, calls=%fused_computation.26 | loop fusion | flops 33554432 | bytes 41981952 | tf_op jit(solution)/shard_map/convert_element_type | solution.py:76
  159.5 2.8 fusion.34
  162.3 1.9 convolution_add_fusion.6
  164.2 0.0 copy-done
  164.3 0.0 copy-done.4
  164.3 0.0 copy-done.2
  164.3 0.0 copy-done.7
  164.3 0.7 convolution_add_fusion.5
  165.0 1.5 convolution_add_fusion.4
  166.6 0.0 reduce-scatter.3.cloned.1.call-update
  166.6 0.0 reduce-scatter.5.cloned.1.call-start
  166.6 7.8 %scatter_custom_fusion = f32[8193,256]{1,0:T(8,128)} fusion(s32[512]{0:T(512)S(1)} %get-tuple-element.20, f32[]{:T(128)} %constant.11.clone.1, bf16[512,256]{1,0:T(8,128)(2,1)} %copy-done.9), kind=kCustom, calls=%fused_computation.10 | custom fusion | flops 262144 | bytes 8651780 | tf_op jit(solution)/shard_map/scatter-add | solution.py:64
  174.4 3.4 %slice-done = f32[8192,256]{1,0:T(8,128)S(1)} async-done(((f32[8193,256]{1,0:T(8,128)}), f32[8192,256]{1,0:T(8,128)S(1)}, s32[]{:S(2)}) %slice-start) | async-done | bytes 8388632 | tf_op jit(solution)/shard_map/slice | solution.py:64
  177.8 1.9 fusion.25
  179.7 2.5 convolution_add_fusion.2
  182.3 0.8 convolution_add_fusion.1
  183.0 0.8 copy-done.1
  183.9 0.7 convolution_add_fusion.3
  184.6 0.8 convolution_add_fusion
  185.4 0.8 pad_maximum_fusion
  186.2 3.8 %copy.8 = f32[4,4,512,256]{3,2,1,0:T(8,128)} copy(f32[4,4,512,256]{3,2,0,1:T(8,128)S(1)} %pad_maximum_fusion) | data formatting | bytes 16777216 | tf_op jit(solution)/shard_map/concatenate | solution.py:83
  190.0 0.0 reduce-scatter.5.cloned.1.call-update
  190.1 0.6 dynamic_slice.3
  190.6 36.7 %reduce-scatter.3.cloned.1.call-done = f32[64,256]{1,0:T(8,128)} async-done(((f32[512,256]{1,0:T(8,128)}), f32[64,256]{1,0:T(8,128)}) %reduce-scatter.3.cloned.1.call-update) | async-done | bytes 65552 | tf_op jit(solution)/shard_map/reduce_scatter | solution.py:85
  227.3 1.5 convert_element_type.38
  228.8 72.7 %reduce-scatter.5.cloned.1.call-done = f32[2048,256]{1,0:T(8,128)} async-done(((f32[8192,256]{1,0:T(8,128)}), f32[2048,256]{1,0:T(8,128)}) %reduce-scatter.5.cloned.1.call-update) | async-done | bytes 2097168 | tf_op jit(solution)/shard_map/reduce_scatter | solution.py:84
  (31 shorter events, 0.1 us)
Async XLA Ops:
  7.2 220.2 %reduce-scatter.3.cloned.1.call-start = ((), (), s32[]{:S(2)}) async-start(), calls=%async_computation.2 | async-start | bytes 589824 | tf_op jit(solution)/shard_map/reduce_scatter | solution.py:85
  70.9 14.3 %copy-start.9 = (bf16[512,256]{1,0:T(8,128)(2,1)}, bf16[512,256]{1,0:T(8,128)(2,1)S(1)}, u32[]{:S(2)}) copy-start(bf16[512,256]{1,0:T(8,128)(2,1)S(1)} %all_gather.7) | copy-start | bytes 786436
  74.5 8.1 %copy-start.8 = (bf16[4,1,512,256]{3,2,1,0:T(8,128)(2,1)}, bf16[4,1,512,256]{3,2,1,0:T(8,128)(2,1)S(1)}, u32[]{:S(2)}) copy-start(bf16[4,1,512,256]{3,2,1,0:T(8,128)(2,1)S(1)} %get-tuple-element.29) | copy-start | bytes 3145732
  74.5 13.5 %copy-start.6 = (bf16[4,1,512,256]{3,2,1,0:T(8,128)(2,1)}, bf16[4,1,512,256]{3,2,1,0:T(8,128)(2,1)S(1)}, u32[]{:S(2)}) copy-start(bf16[4,1,512,256]{3,2,1,0:T(8,128)(2,1)S(1)} %get-tuple-element.31) | copy-start | bytes 3145732
  85.2 5.7 %copy-start.11 = (bf16[4,1,512,256]{3,2,1,0:T(8,128)(2,1)S(1)}, bf16[4,1,512,256]{3,2,1,0:T(8,128)(2,1)}, u32[]{:S(2)}) copy-start(bf16[4,1,512,256]{3,2,1,0:T(8,128)(2,1)} %get-tuple-element.32) | copy-start | bytes 3145732
  90.7 24.5 %copy-start.12 = (s32[512]{0:T(512)S(1)}, s32[512]{0:T(512)}, u32[]{:S(2)}) copy-start(s32[512]{0:T(512)} %param.6) | copy-start | bytes 6148
  90.7 24.5 %copy-start.10 = (bf16[512,256]{1,0:T(8,128)(2,1)S(1)}, bf16[512,256]{1,0:T(8,128)(2,1)}, u32[]{:S(2)}) copy-start(bf16[512,256]{1,0:T(8,128)(2,1)} %copy-done.9) | copy-start | bytes 786436
  159.4 4.8 %copy-start = (bf16[512,2048]{1,0:T(8,128)(2,1)}, bf16[512,2048]{1,0:T(8,128)(2,1)S(1)}, u32[]{:S(2)}) copy-start(bf16[512,2048]{1,0:T(8,128)(2,1)S(1)} %get-tuple-element.38) | copy-start | bytes 6291460
  159.4 4.8 %copy-start.4 = (bf16[512,2048]{1,0:T(8,128)(2,1)}, bf16[512,2048]{1,0:T(8,128)(2,1)S(1)}, u32[]{:S(2)}) copy-start(bf16[512,2048]{1,0:T(8,128)(2,1)S(1)} %get-tuple-element.36) | copy-start | bytes 6291460
  159.4 4.8 %copy-start.2 = (bf16[512,2048]{1,0:T(8,128)(2,1)}, bf16[512,2048]{1,0:T(8,128)(2,1)S(1)}, u32[]{:S(2)}) copy-start(bf16[512,2048]{1,0:T(8,128)(2,1)S(1)} %get-tuple-element.37) | copy-start | bytes 6291460
  159.4 4.8 %copy-start.7 = (bf16[4,1,512,256]{3,2,1,0:T(8,128)(2,1)S(1)}, bf16[4,1,512,256]{3,2,1,0:T(8,128)(2,1)}, u32[]{:S(2)}) copy-start(bf16[4,1,512,256]{3,2,1,0:T(8,128)(2,1)} %copy-done.6) | copy-start | bytes 3145732
  166.6 134.9 %reduce-scatter.5.cloned.1.call-start = ((), (), s32[]{:S(2)}) async-start(), calls=%async_computation.3 | async-start | bytes 10485760 | tf_op jit(solution)/shard_map/reduce_scatter | solution.py:84
  174.4 3.4 %slice-start = ((f32[8193,256]{1,0:T(8,128)}), f32[8192,256]{1,0:T(8,128)S(1)}, s32[]{:S(2)}) async-start(f32[8193,256]{1,0:T(8,128)} %scatter_custom_fusion), calls=%async_computation.4 | async-start | bytes 16777216 | tf_op jit(solution)/shard_map/slice | solution.py:64
  177.8 1.9 copy-start.5
  179.7 2.5 copy-start.3
  182.3 1.6 copy-start.1
Sparse Core Ops, SparseCore 0:
  166.7 60.6 reduce-scatter.2
  230.7 70.7 reduce-scatter.4
where the time goes:
time: 309 us; the launch traced here: 308 us
  waiting for transfers between devices  109 us (35%)
  blocking collectives  103 us (33%)
  matrix products  43.9 us (14%)
  other arithmetic  23.9 us (8%)
  between operations  14.3 us (5%)
  local copies, waits for them, and re-layouts  14.1 us (5%)
    reduce_scatter x1, waiting for transfers between devices, per_device(): lax.psum_scatter(whole, 'dp', scatter_dimension=0, tiled=True)  72.7 us
    reduce_scatter x1, waiting for transfers between devices, per_device(): lax.psum_scatter(lat_grad, 'code', scatter_dimension=0, tiled=True)  36.7 us
    all_gather x1, blocking collectives, per_device(): lax.all_gather(latents, 'code', axis=0, tiled=True)  32.8 us
    all_gather x1, blocking collectives, per_device(): lax.all_gather(out_grad, 'code', axis=0, tiled=True)  30.9 us
    pmax x1, blocking collectives, per_device(): peak_value = lax.pmax(top, 'code')  21.4 us
    dot_general x4, matrix products, block_parts(): lax.dot_general(grad_all, book_block, dims_nt, preferred_element_type=jnp...  21.2 us
    psum x1, blocking collectives, per_device(): lax.psum((total * rescale, weighted * rescale, picked), 'code')  17.5 us
    convert_element_type x1, other arithmetic, per_device(): delta = delta.astype(jnp.bfloat16)  13.5 us
  transfers between devices with their start and end apart: 2, of which 2 were waited for; matrix products, arithmetic and copies ran while one was open for 7% of the time, Pallas kernels for 0%

commit v1 on v0

v1 whole, which is shorter than its diff:
```python
import functools

import jax
import jax.numpy as jnp
from jax import lax
from jax.experimental import pallas as pl
from jax.experimental.pallas import tpu as pltpu
from jax.sharding import PartitionSpec as P

F32 = jnp.float32
BF16 = jnp.bfloat16
CORES = 2


def dims_of(dp, code):
    nx = dp // CORES
    ny = 2 if code % 2 == 0 else 1
    return nx, ny, code // ny


def kernel(
    dims, lat_ref, grad_ref, tgt_ref, book_ref, lg_ref, cg_ref, loss_ref,
    tok, tg, book, book_t, expo, back, delta, tops, sums, stats, stats_in,
    other, other_in, lgrad, lgrad_x, lgrad_y, lgrad_z, acc, ssem, rsem, lsem,
):
    nx, ny, nz, kb = dims
    own, width = lat_ref.shape
    groups = nx * ny
    wide = nz * own
    sub = cg_ref.shape[0]
    codes = CORES * sub
    blocks = codes // kb
    half_blocks = sub // kb
    dp = lax.axis_index("dp")
    code = lax.axis_index("code")
    x, core = dp // CORES, dp % CORES
    z, y = code // ny, code % ny

    def at(dx=0, dy=0, dz=0):
        return (
            lax.rem(x + dx + nx, nx) * CORES + core,
            lax.rem(z + dz + nz, nz) * ny + lax.rem(y + dy + ny, ny),
        )

    mate = (x * CORES + (1 - core), code)
    used = [0]

    def send(src, dst, device):
        i = used[0]
        used[0] += 1
        return pltpu.make_async_remote_copy(
            src_ref=src, dst_ref=dst, send_sem=ssem.at[i], recv_sem=rsem.at[i],
            device_id=device, device_id_type=pl.DeviceIdType.MESH,
        )

    first_code = code * book_ref.shape[0]
    bases = (
        first_code + (x * CORES + (1 - core)) * sub,
        first_code + dp * sub,
    )
    loads = []
    for half, row in enumerate((1 - core, core)):
        start = pl.multiple_of((x * CORES + row) * sub, sub)
        load = pltpu.make_async_copy(
            book_ref.at[pl.ds(start, sub)], book.at[pl.ds(half * sub, sub)], lsem.at[half]
        )
        load.start()
        loads.append(load)

    tok[0:own, 0:width] = lat_ref[...]
    tok[0:own, width:] = grad_ref[...]
    for ry in range(ny):
        tg[ry] = tgt_ref[ry]

    barrier = pltpu.get_barrier_semaphore()
    partners = [at(dx=k) for k in range(1, nx)] + [at(dy=k) for k in range(1, ny)]
    partners += [at(dz=k) for k in range(1, nz)] + [mate]
    for partner in partners:
        pl.semaphore_signal(barrier, inc=1, device_id=partner, device_id_type=pl.DeviceIdType.MESH)
    pl.semaphore_wait(barrier, len(partners))

    def rows(rx, ry, rz):
        return pl.ds(((rx * ny + ry) * nz + rz) * own, own)

    pending = []

    def launch(copy):
        copy.start()
        pending.append(copy)
        return copy

    z_in = {
        k: launch(send(tok.at[rows(0, 0, 0)], tok.at[rows(0, 0, k)], at(dz=-k)))
        for k in range(1, nz)
    }
    x_in, y_in = {}, {}

    def forward_x(ry, rz):
        for k in range(1, nx):
            x_in[k, ry, rz] = launch(
                send(tok.at[rows(0, ry, rz)], tok.at[rows(k, ry, rz)], at(dx=-k))
            )

    def forward_y(rz):
        for k in range(1, ny):
            y_in[k, rz] = launch(
                send(tok.at[rows(0, 0, rz)], tok.at[rows(0, k, rz)], at(dy=-k))
            )

    forward_x(0, 0)
    forward_y(0)
    tg_in = {
        k: launch(send(tg.at[pl.ds(0, ny)], tg.at[pl.ds(k * ny, ny)], at(dx=-k)))
        for k in range(1, nx)
    }
    for rz in range(1, nz):
        z_in[rz].wait_recv()
        forward_x(0, rz)
        forward_y(rz)
    for load in loads:
        load.wait()

    nt = (((1,), (1,)), ((), ()))

    def base_of(b):
        return jnp.where(b < half_blocks, bases[0] + b * kb, bases[1] + (b - half_blocks) * kb)

    def hits(g, b):
        ids = lax.broadcasted_iota(jnp.int32, (kb, wide), 0)
        return ids == (tg[g] - base_of(b))

    def first_pass(g):
        lat_g = tok[g * wide : (g + 1) * wide, 0:width]
        grad_g = tok[g * wide : (g + 1) * wide, width:]

        def body(b, carry):
            here = pl.ds(pl.multiple_of(b * kb, kb), kb)
            part = book[here, :]
            logit = lax.dot_general(part, lat_g, nt, preferred_element_type=F32)
            bk = lax.dot_general(part, grad_g, nt, preferred_element_type=F32)
            top = jnp.max(logit, axis=0, keepdims=True)
            ex = jnp.exp(logit - top)
            expo[g, here, :] = ex
            back[g, here, :] = bk
            tops[g, pl.ds(b, 1), :] = top
            sums[0, pl.ds(b, 1), :] = jnp.sum(ex, axis=0, keepdims=True)
            sums[1, pl.ds(b, 1), :] = jnp.sum(ex * bk, axis=0, keepdims=True)
            sums[2, pl.ds(b, 1), :] = jnp.sum(
                jnp.where(hits(g, b), logit, 0.0), axis=0, keepdims=True
            )
            return carry

        lax.fori_loop(0, blocks, body, 0, unroll=2)
        block_tops = tops[g]
        top = jnp.max(block_tops, axis=0, keepdims=True)
        factor = jnp.exp(block_tops - top)
        stats[0, g, 0:1, :] = top
        stats[0, g, 1:2, :] = jnp.sum(sums[0] * factor, axis=0, keepdims=True)
        stats[0, g, 2:3, :] = jnp.sum(sums[1] * factor, axis=0, keepdims=True)
        stats[0, g, 3:4, :] = jnp.sum(sums[2], axis=0, keepdims=True)
        stats[0, g, 4:8, :] = jnp.zeros((4, wide), F32)

    first_pass(0)
    for k in range(1, ny):
        for rz in range(nz):
            y_in[k, rz].wait_recv()
            forward_x(k, rz)
    for ry in range(1, ny):
        first_pass(ry)
    for b in range(blocks):
        book_t[:, b * kb : (b + 1) * kb] = book[b * kb : (b + 1) * kb, :].T
    for k in range(1, nx):
        tg_in[k].wait_recv()
        for ry in range(ny):
            for rz in range(nz):
                x_in[k, ry, rz].wait_recv()
            first_pass(k * ny + ry)

    def merge(mine, theirs):
        top = jnp.maximum(mine[0:1], theirs[0:1])
        fm, ft = jnp.exp(mine[0:1] - top), jnp.exp(theirs[0:1] - top)
        return jnp.concatenate(
            [
                top,
                mine[1:2] * fm + theirs[1:2] * ft,
                mine[2:3] * fm + theirs[2:3] * ft,
                mine[3:4] + theirs[3:4],
                jnp.zeros((4, wide), F32),
            ],
            axis=0,
        )

    def direct_part(lo, hi):
        def body(b, carry):
            here = pl.ds(pl.multiple_of(b * kb, kb), kb)
            total = None
            for g in range(groups):
                onehot = hits(g, b).astype(F32).astype(BF16)
                term = jnp.dot(
                    onehot, tok[g * wide : (g + 1) * wide, width:], preferred_element_type=F32
                )
                total = term if total is None else total + term
            if lo == 0:
                other[here, :] = total
            else:
                cg_ref[pl.ds(pl.multiple_of((b - half_blocks) * kb, kb), kb), :] = total
            return carry

        lax.fori_loop(lo, hi, body, 0)

    slot = 0
    stages = [("x", nx), ("y", ny), ("z", nz)]
    for s, (axis, n) in enumerate(stages):
        arrivals = []
        for k in range(1, n):
            to = at(**{"d" + axis: -k})
            arrivals.append((k, slot, launch(send(stats.at[s], stats_in.at[slot], to))))
            slot += 1
        if s == 0:
            direct_part(0, half_blocks)
        if s == 1:
            direct_part(half_blocks, blocks)
        for _, _, copy in arrivals:
            copy.wait_recv()
        for g in range(groups):
            rx, ry = g // ny, g % ny
            value = stats[s, g]
            for k, place, _ in arrivals:
                if axis == "x":
                    theirs = stats_in[place, ((rx - k) % nx) * ny + ry]
                elif axis == "y":
                    theirs = stats_in[place, rx * ny + (ry - k) % ny]
                else:
                    theirs = pltpu.roll(stats_in[place, g], k * own, 1)
                value = merge(value, theirs)
            stats[s + 1, g] = value
    final = len(stages)
    top = stats[final, 0, 0:1, :]
    loss = top + jnp.log(stats[final, 0, 1:2, :]) - stats[final, 0, 3:4, :]
    loss_ref[...] = loss[:, 0:own]

    def second_pass(g):
        lse = stats[final, g, 0:1, :] + jnp.log(stats[final, g, 1:2, :])
        shift = 1.0 - stats[final, g, 2:3, :] / stats[final, g, 1:2, :]
        acc[...] = jnp.zeros_like(acc)

        def body(b, carry):
            here = pl.ds(pl.multiple_of(b * kb, kb), kb)
            scale = jnp.exp(tops[g, pl.ds(b, 1), :] - lse)
            probs = expo[g, here, :] * scale
            value = probs * (back[g, here, :] + shift)
            value = value - jnp.where(hits(g, b), 1.0, 0.0)
            value = value.astype(BF16)
            delta[here, g * wide : (g + 1) * wide] = value
            acc[...] += jnp.dot(book_t[:, here], value, preferred_element_type=F32)
            return carry

        lax.fori_loop(0, blocks, body, 0, unroll=2)
        lgrad[g * wide : (g + 1) * wide, :] = acc[...].T.astype(BF16)

    lx_in, ly_in, lz_in = {}, {}, {}
    for k in range(1, nx):
        for ry in reversed(range(ny)):
            g = k * ny + ry
            second_pass(g)
            lx_in[k, ry] = launch(
                send(
                    lgrad.at[pl.ds(g * wide, wide)],
                    lgrad_x.at[pl.ds(((k - 1) * ny + ry) * wide, wide)],
                    at(dx=k),
                )
            )
    for ry in reversed(range(ny)):
        second_pass(ry)

    def sum_x(ry):
        value = lgrad[ry * wide : (ry + 1) * wide, :].astype(F32)
        for k in range(1, nx):
            lx_in[k, ry].wait_recv()
            value += lgrad_x[((k - 1) * ny + ry) * wide : ((k - 1) * ny + ry + 1) * wide, :].astype(F32)
        return value

    def book_part(lo, hi, ref):
        def body(b, carry):
            here = pl.ds(pl.multiple_of(b * kb, kb), kb)
            there = pl.ds(pl.multiple_of((b - lo) * kb, kb), kb)
            ref[there, :] += jnp.dot(delta[here, :], tok[:, 0:width], preferred_element_type=F32)
            return carry

        lax.fori_loop(lo, hi, body, 0)

    other_copies = []
    for b in range(half_blocks):
        here = pl.ds(b * kb, kb)
        other[here, :] += jnp.dot(delta[b * kb : (b + 1) * kb, :], tok[:, 0:width], preferred_element_type=F32)
        other_copies.append(launch(send(other.at[here], other_in.at[here], mate)))

    for k in range(1, ny):
        lgrad[k * wide : (k + 1) * wide, :] = sum_x(k).astype(BF16)
        ly_in[k] = launch(
            send(
                lgrad.at[pl.ds(k * wide, wide)],
                lgrad_y.at[pl.ds((k - 1) * wide, wide)],
                at(dy=k),
            )
        )
    mine = sum_x(0)
    acc[...] = mine
    book_part(half_blocks, blocks, cg_ref)

    mine = acc[...]
    for k in range(1, ny):
        ly_in[k].wait_recv()
        mine = mine + lgrad_y[(k - 1) * wide : k * wide, :].astype(F32)
    acc[...] = mine
    lgrad[own:wide, :] = acc[own:wide, :].astype(BF16)
    for k in range(1, nz):
        lz_in[k] = launch(
            send(
                lgrad.at[pl.ds(k * own, own)],
                lgrad_z.at[pl.ds((k - 1) * own, own)],
                at(dz=k),
            )
        )
    for b in range(half_blocks):
        other_copies[b].wait_recv()
        cg_ref[b * kb : (b + 1) * kb, :] += other_in[b * kb : (b + 1) * kb, :]
    mine = acc[0:own, :]
    for k in range(1, nz):
        lz_in[k].wait_recv()
        mine = mine + lgrad_z[(k - 1) * own : k * own, :].astype(F32)
    lg_ref[...] = mine.astype(BF16)
    for copy in pending:
        copy.wait_send()


def per_device(latents, out_grad, targets, codebook):
    own, width = latents.shape
    code_dev = codebook.shape[0]
    dp, code = lax.axis_size("dp"), lax.axis_size("code")
    nx, ny, nz = dims_of(dp, code)
    groups = nx * ny
    wide = nz * own
    sub = code_dev // dp
    codes = CORES * sub
    kb = min(512, sub)
    blocks = codes // kb
    tokens = groups * wide

    place = lax.axis_index("code")
    z, y = place // ny, place % ny
    ordered = targets.reshape(nz, ny, own)
    ordered = lax.dynamic_slice_in_dim(jnp.concatenate([ordered, ordered], 0), z, nz, 0)
    ordered = lax.dynamic_slice_in_dim(jnp.concatenate([ordered, ordered], 1), y, ny, 1)
    ordered = ordered.transpose(1, 0, 2).reshape(ny, 1, wide)

    copies = (nz - 1) + (nx - 1) * (ny * nz + 1) + (ny - 1) * nz
    copies += (nx - 1) + (ny - 1) + (nz - 1)
    copies += (nx - 1) * ny + (ny - 1) + (nz - 1) + sub // kb
    vmem = pl.BlockSpec(memory_space=pltpu.VMEM)
    macs = tokens * codes * width
    lat_out, book_out, loss = pl.pallas_call(
        functools.partial(kernel, (nx, ny, nz, kb)),
        out_shape=(
            jax.ShapeDtypeStruct((own, width), BF16),
            jax.ShapeDtypeStruct((sub, width), F32),
            jax.ShapeDtypeStruct((1, own), F32),
        ),
        in_specs=[vmem, vmem, vmem, pl.BlockSpec(memory_space=pl.ANY)],
        out_specs=(vmem, vmem, vmem),
        scratch_shapes=[
            pltpu.VMEM((tokens, 2 * width), BF16),
            pltpu.VMEM((groups, 1, wide), jnp.int32),
            pltpu.VMEM((codes, width), BF16),
            pltpu.VMEM((width, codes), BF16),
            pltpu.VMEM((groups, codes, wide), F32),
            pltpu.VMEM((groups, codes, wide), F32),
            pltpu.VMEM((codes, tokens), BF16),
            pltpu.VMEM((groups, blocks, wide), F32),
            pltpu.VMEM((3, blocks, wide), F32),
            pltpu.VMEM((4, groups, 8, wide), F32),
            pltpu.VMEM((max(1, nx + ny + nz - 3), groups, 8, wide), F32),
            pltpu.VMEM((sub, width), F32),
            pltpu.VMEM((sub, width), F32),
            pltpu.VMEM((tokens, width), BF16),
            pltpu.VMEM((max(1, nx - 1) * ny * wide, width), BF16),
            pltpu.VMEM((max(1, ny - 1) * wide, width), BF16),
            pltpu.VMEM((max(1, nz - 1) * own, width), BF16),
            pltpu.VMEM((width, wide), F32),
            pltpu.SemaphoreType.DMA((copies,)),
            pltpu.SemaphoreType.DMA((copies,)),
            pltpu.SemaphoreType.DMA((2,)),
        ],
        compiler_params=pltpu.CompilerParams(
            collective_id=0, has_side_effects=True, vmem_limit_bytes=62 * 2**20
        ),
        cost_estimate=pl.CostEstimate(
            flops=10 * macs, bytes_accessed=2 * codes * width, transcendentals=tokens * codes
        ),
    )(latents, out_grad, ordered, codebook)
    return lat_out, book_out, loss.reshape(own)


def solution(mesh):
    in_specs = (P(("dp", "code"), None), P(("dp", "code"), None), P("dp"), P("code", None))
    out_specs = (P(("dp", "code"), None), P(("code", "dp"), None), P(("dp", "code")))
    return jax.shard_map(
        per_device, mesh=mesh, in_specs=in_specs, out_specs=out_specs, check_vma=False
    )
```

time: 309 us -> 65.9 us (0.21)
  waiting for transfers between devices: 109 us -> 0 us
  blocking collectives: 103 us -> 0 us
  Pallas kernels: 0 us -> 58.5 us
  matrix products: 43.9 us -> 0 us
  other arithmetic: 23.9 us -> 0.04 us
  between operations: 14.3 us -> 0.69 us
  local copies, waits for them, and re-layouts: 14.1 us -> 6.36 us
    reduce_scatter x2 -> x0, waiting for transfers between devices: 109 us -> none  [the longest x1 72.7 us: per_device(): lax.psum_scatter(whole, 'dp', scatter_dimension=0, tiled=True)]
    all_gather x2 -> x0, blocking collectives: 63.7 us -> none  [the longest x1 32.8 us: per_device(): lax.all_gather(latents, 'code', axis=0, tiled=True)]
    pallas_call x0 -> x1, Pallas kernels: none -> 58.5 us  [per_device(): pl.pallas_call(functools.partial(kernel, (nx, ny, nz, kb)), out_shape=(ja...]
    dot_general x16 -> x0, matrix products: 43.9 us -> none  [the longest x4 21.2 us: block_parts(): lax.dot_general(grad_all, book_block, dims_nt, preferred_element_type=jnp...]
    pmax x1 -> x0, blocking collectives: 21.4 us -> none  [per_device(): peak_value = lax.pmax(top, 'code')]
    psum x1 -> x0, blocking collectives: 17.5 us -> none  [per_device(): lax.psum((total * rescale, weighted * rescale, picked), 'code')]
    convert_element_type x2 -> x0, other arithmetic: 15 us -> none  [the longest x1 13.5 us: per_device(): delta = delta.astype(jnp.bfloat16)]
    slice x4 -> x0, local copies, waits for them, and re-layouts: 8.79 us -> none  [the longest x1 3.51 us: block_parts(): book_block = layered[:, block].reshape(groups * block_rows, feature_width)]
  transfers between devices with their start and end apart: 2 -> 0, of which waited for: 2 -> 0; matrix products, arithmetic and copies ran while one was open for 7% -> 0% of each run, Pallas kernels for 0% -> 0%
where the time goes in v1:
time: 65.9 us; the launch traced here: 65.5 us
  Pallas kernels  58.5 us (89%)
  local copies, waits for them, and re-layouts  6.36 us (10%)
  between operations  0.69 us (1%)
    pallas_call x1, Pallas kernels, per_device(): pl.pallas_call(functools.partial(kernel, (nx, ny, nz, kb)), out_shape=(ja...  58.5 us
    unnamed x5, local copies, waits for them, and re-layouts  4.94 us

profile of v1, /device:TPU:0, one launch (start us, length us, event | category | flops | bytes accessed | tf_op | source)
XLA Modules:
  0.0 65.5 jit_solution(1011956031124971760)
XLA Ops:
  0.7 0.8 %reshape.15 = s32[4,2,64]{2,1,0:T(2,128)S(1)} reshape(s32[512]{0:T(512)} %param.6) | data formatting | bytes 4096 | tf_op jit(solution)/shard_map/reshape | solution.py:352
  1.5 0.7 %reshape.16.tgt_ref = s32[2,1,256]{2,1,0:T(1,128)} reshape(s32[2,4,64]{2,1,0:T(4,128)S(1)} %copy.7) | data formatting | bytes 4096 | tf_op jit(solution)/shard_map/reshape | solution.py:355
  2.1 58.5 %shard_map.67 = (bf16[64,256]{1,0:T(8,128)(2,1)}, f32[2048,256]{1,0:T(8,128)}, f32[1,64]{1,0:T(1,128)}) custom-call(bf16[64,256]{1,0:T(8,128)(2,1)} %lat_ref.1, bf16[64,256]{1,0:T(8,128)(2,1)} %grad_ref.1, s32[2,1,256]{2,1,0:T(1,128)} %reshape.16.tgt_ref, bf16[8192,256]{1,0:T(8,128)(2,1)} %book_ref.1), custom_call_target="tpu_custom_call" | custom-call | flops 10737418240 | bytes 2097152 | tf_op jit(solution)/shard_map/pallas_call | solution.py:362
  60.6 1.4 %copy.11 = bf16[64,256]{1,0:T(8,128)(2,1)} copy(bf16[64,256]{1,0:T(8,128)(2,1)} %get-tuple-element.12) | data formatting | bytes 65536
  62.0 0.0 copy-start
  62.0 3.0 %copy.12 = f32[2048,256]{1,0:T(8,128)} copy(f32[2048,256]{1,0:T(8,128)} %get-tuple-element.13) | data formatting | bytes 4194304
  65.0 0.0 copy-done
  65.0 0.5 copy.13
  (3 shorter events, 0.0 us)
Async XLA Ops:
  62.0 3.0 %copy-start = (f32[1,64]{1,0:T(1,128)S(1)}, f32[1,64]{1,0:T(1,128)}, u32[]{:S(2)}) copy-start(f32[1,64]{1,0:T(1,128)} %get-tuple-element.8) | copy-start | bytes 772

commit v2 on v1

--- a/solution.py
+++ b/solution.py
@@ -19,15 +19,15 @@
 
 
 def kernel(
-    dims, lat_ref, grad_ref, tgt_ref, book_ref, lg_ref, cg_ref, loss_ref,
+    dims, lat_ref, grad_ref, tgt_ref, book_ref, lg_ref, mine_ref, theirs_ref, loss_ref,
     tok, tg, book, book_t, expo, back, delta, tops, sums, stats, stats_in,
-    other, other_in, lgrad, lgrad_x, lgrad_y, lgrad_z, acc, ssem, rsem, lsem,
+    other, same, lgrad, lgrad_x, lgrad_y, lgrad_z, acc, ssem, rsem, lsem,
 ):
     nx, ny, nz, kb = dims
     own, width = lat_ref.shape
     groups = nx * ny
     wide = nz * own
-    sub = cg_ref.shape[0]
+    sub = mine_ref.shape[0]
     codes = CORES * sub
     blocks = codes // kb
     half_blocks = sub // kb
@@ -69,18 +69,18 @@
 
     tok[0:own, 0:width] = lat_ref[...]
     tok[0:own, width:] = grad_ref[...]
-    for ry in range(ny):
-        tg[ry] = tgt_ref[ry]
-
     barrier = pltpu.get_barrier_semaphore()
-    partners = [at(dx=k) for k in range(1, nx)] + [at(dy=k) for k in range(1, ny)]
+    square = [(kx, ky) for kx in range(nx) for ky in range(ny)][1:]
+    partners = [at(dx=kx, dy=ky) for kx, ky in square]
     partners += [at(dz=k) for k in range(1, nz)] + [mate]
     for partner in partners:
         pl.semaphore_signal(barrier, inc=1, device_id=partner, device_id_type=pl.DeviceIdType.MESH)
     pl.semaphore_wait(barrier, len(partners))
 
-    def rows(rx, ry, rz):
-        return pl.ds(((rx * ny + ry) * nz + rz) * own, own)
+    cut = own // 2 if ny > 1 and own % 32 == 0 else own
+
+    def rows(rx, ry, rz, lo=0, hi=own):
+        return pl.ds(((rx * ny + ry) * nz + rz) * own + lo, hi - lo)
 
     pending = []
 
@@ -93,12 +93,23 @@
         k: launch(send(tok.at[rows(0, 0, 0)], tok.at[rows(0, 0, k)], at(dz=-k)))
         for k in range(1, nz)
     }
-    x_in, y_in = {}, {}
+    x_in, y_in, xy_in = {}, {}, {}
 
     def forward_x(ry, rz):
         for k in range(1, nx):
+            hi = cut if ry else own
             x_in[k, ry, rz] = launch(
-                send(tok.at[rows(0, ry, rz)], tok.at[rows(k, ry, rz)], at(dx=-k))
+                send(tok.at[rows(0, ry, rz, 0, hi)], tok.at[rows(k, ry, rz, 0, hi)], at(dx=-k))
+            )
+
+    def forward_xy(k, rz):
+        if cut == own:
+            return
+        for ky in range(1, ny):
+            xy_in[k, ky, rz] = launch(
+                send(
+                    tok.at[rows(k, 0, rz, cut)], tok.at[rows(k, ky, rz, cut)], at(dy=-ky)
+                )
             )
 
     def forward_y(rz):
@@ -109,6 +120,17 @@
 
     forward_x(0, 0)
     forward_y(0)
+    everyone = jnp.broadcast_to(tgt_ref[...], (8, nz * ny * own))
+    lane = lax.broadcasted_iota(jnp.int32, (8, nz * ny * own), 1)
+    for ry in range(ny):
+        line = everyone
+        for rz in range(nz):
+            owner = lax.rem(z + rz, nz) * ny + lax.rem(y + ry, ny)
+            turn = lax.rem(rz - owner + nz * ny, nz * ny) * own
+            line = jnp.where(lane >= rz * own, pltpu.roll(everyone, turn, 1), line) if rz else (
+                pltpu.roll(everyone, turn, 1)
+            )
+        tg[ry] = line[0:1, 0:wide]
     tg_in = {
         k: launch(send(tg.at[pl.ds(0, ny)], tg.at[pl.ds(k * ny, ny)], at(dx=-k)))
         for k in range(1, nx)
@@ -158,13 +180,16 @@
         stats[0, g, 1:2, :] = jnp.sum(sums[0] * factor, axis=0, keepdims=True)
         stats[0, g, 2:3, :] = jnp.sum(sums[1] * factor, axis=0, keepdims=True)
         stats[0, g, 3:4, :] = jnp.sum(sums[2], axis=0, keepdims=True)
-        stats[0, g, 4:8, :] = jnp.zeros((4, wide), F32)
 
     first_pass(0)
     for k in range(1, ny):
         for rz in range(nz):
             y_in[k, rz].wait_recv()
             forward_x(k, rz)
+    for k in range(1, nx):
+        for rz in range(nz):
+            x_in[k, 0, rz].wait_recv()
+            forward_xy(k, rz)
     for ry in range(1, ny):
         first_pass(ry)
     for b in range(blocks):
@@ -173,7 +198,10 @@
         tg_in[k].wait_recv()
         for ry in range(ny):
             for rz in range(nz):
-                x_in[k, ry, rz].wait_recv()
+                if ry:
+                    x_in[k, ry, rz].wait_recv()
+                    if cut < own:
+                        xy_in[k, ry, rz].wait_recv()
             first_pass(k * ny + ry)
 
     def merge(mine, theirs):
@@ -185,7 +213,6 @@
                 mine[1:2] * fm + theirs[1:2] * ft,
                 mine[2:3] * fm + theirs[2:3] * ft,
                 mine[3:4] + theirs[3:4],
-                jnp.zeros((4, wide), F32),
             ],
             axis=0,
         )
@@ -203,35 +230,34 @@
             if lo == 0:
                 other[here, :] = total
             else:
-                cg_ref[pl.ds(pl.multiple_of((b - half_blocks) * kb, kb), kb), :] = total
+                same[pl.ds(pl.multiple_of((b - half_blocks) * kb, kb), kb), :] = total
             return carry
 
         lax.fori_loop(lo, hi, body, 0)
 
     slot = 0
-    stages = [("x", nx), ("y", ny), ("z", nz)]
-    for s, (axis, n) in enumerate(stages):
+    stages = [square, [(k,) for k in range(1, nz)]]
+    for s, peers in enumerate(stages):
         arrivals = []
-        for k in range(1, n):
-            to = at(**{"d" + axis: -k})
-            arrivals.append((k, slot, launch(send(stats.at[s], stats_in.at[slot], to))))
+        for peer in peers:
+            to = at(-peer[0], -peer[1]) if s == 0 else at(dz=-peer[0])
+            copy = launch(send(stats.at[s], stats_in.at[slot], to))
+            arrivals.append((peer, slot, copy))
             slot += 1
         if s == 0:
             direct_part(0, half_blocks)
-        if s == 1:
+        else:
             direct_part(half_blocks, blocks)
         for _, _, copy in arrivals:
             copy.wait_recv()
         for g in range(groups):
             rx, ry = g // ny, g % ny
             value = stats[s, g]
-            for k, place, _ in arrivals:
-                if axis == "x":
-                    theirs = stats_in[place, ((rx - k) % nx) * ny + ry]
-                elif axis == "y":
-                    theirs = stats_in[place, rx * ny + (ry - k) % ny]
+            for peer, place, _ in arrivals:
+                if s == 0:
+                    theirs = stats_in[place, ((rx - peer[0]) % nx) * ny + (ry - peer[1]) % ny]
                 else:
-                    theirs = pltpu.roll(stats_in[place, g], k * own, 1)
+                    theirs = pltpu.roll(stats_in[place, g], peer[0] * own, 1)
                 value = merge(value, theirs)
             stats[s + 1, g] = value
     final = len(stages)
@@ -280,20 +306,11 @@
             value += lgrad_x[((k - 1) * ny + ry) * wide : ((k - 1) * ny + ry + 1) * wide, :].astype(F32)
         return value
 
-    def book_part(lo, hi, ref):
-        def body(b, carry):
-            here = pl.ds(pl.multiple_of(b * kb, kb), kb)
-            there = pl.ds(pl.multiple_of((b - lo) * kb, kb), kb)
-            ref[there, :] += jnp.dot(delta[here, :], tok[:, 0:width], preferred_element_type=F32)
-            return carry
-
-        lax.fori_loop(lo, hi, body, 0)
-
     other_copies = []
     for b in range(half_blocks):
         here = pl.ds(b * kb, kb)
         other[here, :] += jnp.dot(delta[b * kb : (b + 1) * kb, :], tok[:, 0:width], preferred_element_type=F32)
-        other_copies.append(launch(send(other.at[here], other_in.at[here], mate)))
+        other_copies.append(launch(send(other.at[here], theirs_ref.at[here], mate)))
 
     for k in range(1, ny):
         lgrad[k * wide : (k + 1) * wide, :] = sum_x(k).astype(BF16)
@@ -306,29 +323,36 @@
         )
     mine = sum_x(0)
     acc[...] = mine
-    book_part(half_blocks, blocks, cg_ref)
+    stores = []
+    for b in range(half_blocks):
+        here = pl.ds(b * kb, kb)
+        same[here, :] += jnp.dot(
+            delta[sub + b * kb : sub + (b + 1) * kb, :], tok[:, 0:width], preferred_element_type=F32
+        )
+        store = pltpu.make_async_copy(same.at[here], mine_ref.at[here], lsem.at[2 + b])
+        store.start()
+        stores.append(store)
 
     mine = acc[...]
     for k in range(1, ny):
         ly_in[k].wait_recv()
         mine = mine + lgrad_y[(k - 1) * wide : k * wide, :].astype(F32)
     acc[...] = mine
-    lgrad[own:wide, :] = acc[own:wide, :].astype(BF16)
     for k in range(1, nz):
         lz_in[k] = launch(
             send(
-                lgrad.at[pl.ds(k * own, own)],
+                acc.at[pl.ds(k * own, own)],
                 lgrad_z.at[pl.ds((k - 1) * own, own)],
                 at(dz=k),
             )
         )
     for b in range(half_blocks):
         other_copies[b].wait_recv()
-        cg_ref[b * kb : (b + 1) * kb, :] += other_in[b * kb : (b + 1) * kb, :]
+        stores[b].wait()
     mine = acc[0:own, :]
     for k in range(1, nz):
         lz_in[k].wait_recv()
-        mine = mine + lgrad_z[(k - 1) * own : k * own, :].astype(F32)
+        mine = mine + lgrad_z[(k - 1) * own : k * own, :]
     lg_ref[...] = mine.astype(BF16)
     for copy in pending:
         copy.wait_send()
@@ -347,27 +371,21 @@
     blocks = codes // kb
     tokens = groups * wide
 
-    place = lax.axis_index("code")
-    z, y = place // ny, place % ny
-    ordered = targets.reshape(nz, ny, own)
-    ordered = lax.dynamic_slice_in_dim(jnp.concatenate([ordered, ordered], 0), z, nz, 0)
-    ordered = lax.dynamic_slice_in_dim(jnp.concatenate([ordered, ordered], 1), y, ny, 1)
-    ordered = ordered.transpose(1, 0, 2).reshape(ny, 1, wide)
-
     copies = (nz - 1) + (nx - 1) * (ny * nz + 1) + (ny - 1) * nz
-    copies += (nx - 1) + (ny - 1) + (nz - 1)
+    copies += (nx * ny - 1) + (nz - 1) + (nx - 1) * (ny - 1) * nz
     copies += (nx - 1) * ny + (ny - 1) + (nz - 1) + sub // kb
     vmem = pl.BlockSpec(memory_space=pltpu.VMEM)
     macs = tokens * codes * width
-    lat_out, book_out, loss = pl.pallas_call(
+    lat_out, mine, theirs, loss = pl.pallas_call(
         functools.partial(kernel, (nx, ny, nz, kb)),
         out_shape=(
             jax.ShapeDtypeStruct((own, width), BF16),
             jax.ShapeDtypeStruct((sub, width), F32),
+            jax.ShapeDtypeStruct((sub, width), F32),
             jax.ShapeDtypeStruct((1, own), F32),
         ),
         in_specs=[vmem, vmem, vmem, pl.BlockSpec(memory_space=pl.ANY)],
-        out_specs=(vmem, vmem, vmem),
+        out_specs=(vmem, pl.BlockSpec(memory_space=pl.ANY), pl.BlockSpec(memory_space=pl.ANY), vmem),
         scratch_shapes=[
             pltpu.VMEM((tokens, 2 * width), BF16),
             pltpu.VMEM((groups, 1, wide), jnp.int32),
@@ -378,18 +396,18 @@
             pltpu.VMEM((codes, tokens), BF16),
             pltpu.VMEM((groups, blocks, wide), F32),
             pltpu.VMEM((3, blocks, wide), F32),
-            pltpu.VMEM((4, groups, 8, wide), F32),
-            pltpu.VMEM((max(1, nx + ny + nz - 3), groups, 8, wide), F32),
+            pltpu.VMEM((3, groups, 4, wide), F32),
+            pltpu.VMEM((max(1, nx * ny + nz - 2), groups, 4, wide), F32),
             pltpu.VMEM((sub, width), F32),
             pltpu.VMEM((sub, width), F32),
             pltpu.VMEM((tokens, width), BF16),
             pltpu.VMEM((max(1, nx - 1) * ny * wide, width), BF16),
             pltpu.VMEM((max(1, ny - 1) * wide, width), BF16),
-            pltpu.VMEM((max(1, nz - 1) * own, width), BF16),
+            pltpu.VMEM((max(1, nz - 1) * own, width), F32),
             pltpu.VMEM((width, wide), F32),
             pltpu.SemaphoreType.DMA((copies,)),
             pltpu.SemaphoreType.DMA((copies,)),
-            pltpu.SemaphoreType.DMA((2,)),
+            pltpu.SemaphoreType.DMA((2 + sub // kb,)),
         ],
         compiler_params=pltpu.CompilerParams(
             collective_id=0, has_side_effects=True, vmem_limit_bytes=62 * 2**20
@@ -397,8 +415,26 @@
         cost_estimate=pl.CostEstimate(
             flops=10 * macs, bytes_accessed=2 * codes * width, transcendentals=tokens * codes
         ),
-    )(latents, out_grad, ordered, codebook)
-    return lat_out, book_out, loss.reshape(own)
+    )(latents, out_grad, targets.reshape(1, -1), codebook)
+
+    def finish(lat_ref, mine_ref, theirs_ref, loss_ref, lat_to, book_to, loss_to):
+        book_to[...] = mine_ref[...] + theirs_ref[...]
+        lat_to[...] = lat_ref[...]
+        loss_to[...] = loss_ref[0, :]
+
+    whole_lat = pl.BlockSpec((own, width), lambda i: (0, 0))
+    tile = pl.BlockSpec((kb, width), lambda i: (i, 0))
+    return pl.pallas_call(
+        finish,
+        grid=(sub // kb,),
+        out_shape=(
+            jax.ShapeDtypeStruct((own, width), BF16),
+            jax.ShapeDtypeStruct((sub, width), F32),
+            jax.ShapeDtypeStruct((own,), F32),
+        ),
+        in_specs=[whole_lat, tile, tile, pl.BlockSpec((1, own), lambda i: (0, 0))],
+        out_specs=(whole_lat, tile, pl.BlockSpec((own,), lambda i: (0,))),
+    )(lat_out, mine, theirs, loss)
 
 
 def solution(mesh):

time: 65.9 us -> 61.4 us (0.932)
  local copies, waits for them, and re-layouts: 6.36 us -> 0 us
  Pallas kernels: 58.5 us -> 60.5 us
    unnamed x5 -> x0, local copies, waits for them, and re-layouts: 4.94 us -> none
    pallas_call x0 -> x1, Pallas kernels: none -> 4.2 us  [per_device(): pl.pallas_call(finish, grid=(sub // kb,), out_shape=(jax.ShapeDtypeStruct...]
    pallas_call x1, Pallas kernels: 58.5 us -> 56.3 us  [per_device(): pl.pallas_call(functools.partial(kernel, (nx, ny, nz, kb)), out_shape=(ja...]
    reshape x2 -> x0, local copies, waits for them, and re-layouts: 1.42 us -> none  [the longest x1 0.76 us: per_device(): ordered = targets.reshape(nz, ny, own)]
where the time goes in v2:
time: 61.4 us; the launch traced here: 61.1 us
  Pallas kernels  60.5 us (99%)
  between operations  0.64 us (1%)
    pallas_call x1, Pallas kernels, per_device(): pl.pallas_call(functools.partial(kernel, (nx, ny, nz, kb)), out_shape=(ja...  56.3 us
    pallas_call x1, Pallas kernels, per_device(): pl.pallas_call(finish, grid=(sub // kb,), out_shape=(jax.ShapeDtypeStruct...  4.2 us

profile of v2, /device:TPU:0, one launch (start us, length us, event | category | flops | bytes accessed | tf_op | source)
XLA Modules:
  0.0 61.1 jit_solution(12544649967750989352)
XLA Ops:
  0.6 56.3 %shard_map.67 = (bf16[64,256]{1,0:T(8,128)(2,1)}, f32[2048,256]{1,0:T(8,128)}, f32[2048,256]{1,0:T(8,128)}, f32[1,64]{1,0:T(1,128)}) custom-call(bf16[64,256]{1,0:T(8,128)(2,1)} %lat_ref.1, bf16[64,256]{1,0:T(8,128)(2,1)} %grad_ref.1, s32[1,512]{1,0:T(1,128)} %bitcast.1, bf16[8192,256]{1,0:T(8,128)(2,1)} %book_ref.1), custom_call_target="tpu_custom_call" | custom-call | flops 10737418240 | bytes 2097152 | tf_op jit(solution)/shard_map/pallas_call | solution.py:379
  57.0 4.2 %shard_map.68 = (bf16[64,256]{1,0:T(8,128)(2,1)}, f32[2048,256]{1,0:T(8,128)}, f32[64]{0:T(128)}) custom-call(bf16[64,256]{1,0:T(8,128)(2,1)} %get-tuple-element.7.lat_ref, f32[2048,256]{1,0:T(8,128)} %get-tuple-element.8.mine_ref, f32[2048,256]{1,0:T(8,128)} %get-tuple-element.9.theirs_ref, f32[1,64]{1,0:T(1,128)} %get-tuple-element.10.loss_ref), custom_call_target="tpu_custom_call" | custom-call | tf_op jit(solution)/shard_map/pallas_call | solution.py:427
